TPU v7x, 256 devices: a whole 4x4x8 slice. The times are simulated.
256 devices in a mesh: dp: 32 (over z_lo, y, core), tensor: 8 (over x, z_hi).
Axes of the slice: x: 4, y: 4, z: 8 (z_hi: 2, z_lo: 4; z = z_hi * 4 + z_lo), core: 2. Of those that a mesh axis runs over, the one named last changes fastest.
Arguments:
- hidden_in: bfloat16 [65536, 14336], P('dp', 'tensor'), may hold values from -6 to 6
- grad_out: bfloat16 [65536, 4096], P('dp', 'tensor'), may hold values from -6 to 6
- proj_in: bfloat16 [14336, 64], P('tensor')
- proj_out: bfloat16 [4096, 64], P('tensor')
- lengths: int32 [1024], P('dp'), may hold values from 16 to 64
- store_row: int32 [1024], replicated, may hold values from 0 to 1023, as said below
- queries: bfloat16 [1024, 4096], P('dp', 'tensor'), may hold values from -6 to 6
Outputs:
- store: bfloat16 [1024, 4096], P('dp', 'tensor')
- scores: float32 [1024, 1024], P('dp', 'tensor')
Inputs may be any that keep to these rules, and one draw needn't show every extreme that they name: store_row is a permutation; the sequences of each index of dp are written to every block of 32 consecutive store rows equally often, 32 * 32 / 1024 times.
All inputs are finite; a program needn't handle non-finite values.
Results may differ from a plain program's by a relative error of at most 0.0029.
Values may be sent and summed in bfloat16 or wider, within the bound.
A program may use at most 64 MiB of HBM per device.

v0:
```python
import jax
import jax.numpy as jnp
from jax import lax
from jax.sharding import PartitionSpec as P


def outer_sums(left_fac, right_fac, seq_lengths, length):
    seq_count = seq_lengths.shape[0]
    positions = jnp.arange(length, dtype=jnp.int32)
    live_mask = (positions[None, :] < seq_lengths[:, None]).astype(jnp.float32)
    left_blocks = left_fac.reshape(seq_count, length, -1) * live_mask[:, :, None]
    right_blocks = right_fac.reshape(seq_count, length, -1)
    kron = jnp.einsum("sti,stj->sij", left_blocks, right_blocks, precision=lax.Precision.HIGHEST)
    return kron.reshape(seq_count, -1)


def per_device(hidden_in, grad_out, proj_in, proj_out, lengths, store_row, queries):
    seq_dev = lengths.shape[0]
    proj_rank = proj_in.shape[1]
    length = hidden_in.shape[0] // seq_dev
    tp_count = lax.axis_size("tensor")
    tp_index = lax.axis_index("tensor")
    col_width = proj_rank * proj_rank // tp_count
    in_part = jnp.dot(hidden_in, proj_in, preferred_element_type=jnp.float32)
    out_part = jnp.dot(grad_out, proj_out, preferred_element_type=jnp.float32)
    in_full, out_full = lax.psum((in_part, out_part), "tensor")
    row_band = proj_rank // tp_count
    in_cols = lax.dynamic_slice_in_dim(in_full, tp_index * row_band, row_band, 1)
    kron_cols = outer_sums(in_cols, out_full, lengths, length)
    squares = lax.psum(jnp.sum(kron_cols * kron_cols, axis=1), "tensor")
    inv_norm = 1.0 / jnp.sqrt(squares / (proj_rank * proj_rank) + 1e-06)
    normed = (kron_cols * inv_norm[:, None]).astype(jnp.bfloat16)
    dp_count = lax.axis_size("dp")
    dp_index = lax.axis_index("dp")
    per_pair = seq_dev // dp_count
    own_targets = lax.dynamic_slice_in_dim(store_row, dp_index * seq_dev, seq_dev, 0)
    send_order = jnp.argsort(own_targets // seq_dev, stable=True)
    outgoing = normed[send_order].reshape(dp_count, per_pair, col_width)
    incoming = lax.all_to_all(outgoing, "dp", split_axis=0, concat_axis=0, tiled=True).reshape(
        dp_count * per_pair, col_width
    )
    row_table = store_row.reshape(dp_count, seq_dev)
    arranged = jnp.take_along_axis(
        row_table, jnp.argsort(row_table // seq_dev, axis=1, stable=True), axis=1
    )
    arrived = (
        lax.dynamic_slice_in_dim(arranged, dp_index * per_pair, per_pair, 1).reshape(-1) % seq_dev
    )
    store = jnp.zeros((seq_dev, col_width), jnp.bfloat16).at[arrived].set(incoming)
    partial_value = lax.dot_general(
        store,
        lax.all_gather(queries, "dp", axis=0, tiled=True),
        (((1,), (1,)), ((), ())),
        preferred_element_type=jnp.float32,
    )
    partial_scores = partial_value / proj_rank
    scores = lax.psum_scatter(partial_scores, "tensor", scatter_dimension=1, tiled=True)
    return (store, scores)


def solution(mesh):
    placed = (
        P("dp", "tensor"),
        P("dp", "tensor"),
        P("tensor", None),
        P("tensor", None),
        P("dp"),
        P(),
        P("dp", "tensor"),
    )
    return jax.shard_map(
        per_device,
        mesh=mesh,
        in_specs=placed,
        out_specs=(P("dp", "tensor"), P("dp", "tensor")),
        check_vma=False,
    )
```

profile of v0, /device:TPU:1, one launch (start us, length us, event | category | flops | bytes accessed | tf_op | source)
XLA Modules:
  0.0 316.7 jit_solution(16055053467299210136)
XLA Ops:
  8.0 0.0 copy-start
  8.0 0.0 copy-start.2
  8.0 0.0 all-reduce.3.cloned.1.call-start
  8.1 1.5 copy-done
  9.6 2.5 fusion.12
  12.1 6.2 %fusion.11 = f32[2048,64]{0,1:T(8,128)} fusion(bf16[2048,1792]{1,0:T(8,128)(2,1)} %param.7, bf16[1792,64]{0,1:T(8,128)(2,1)} %param.9), kind=kOutput, calls=%fused_computation.41 | convolution fusion | flops 469762048 | bytes 8093696 | tf_op jit(solution)/shard_map/dot_general | solution.py:24
  18.3 0.0 all-reduce.3.cloned.1.call-update
  18.3 0.0 all-gather.2.cloned.1.call-start
  18.4 0.5 all-gather.2.cloned.1.call-update
  18.9 0.0 copy-done.2
  18.9 0.1 reshape.55
  19.0 0.1 and_select_fusion
  19.1 1.6 sort.35
  20.7 0.1 copy.36
  20.8 0.8 sort.34
  21.6 0.1 copy.40
  21.7 0.1 reshape.70
  21.8 0.0 copy-start.3
  21.8 7.1 %gather_fusion.1 = s32[1024]{0:T(1024)S(1)} fusion(s32[32,32]{1,0:T(8,128)S(1)} %reshape.55, s32[1024]{0:T(1024)S(1)} %reshape.70), kind=kCustom, calls=%fused_computation.1 | custom fusion | bytes 16384 | tf_op jit(solution)/shard_map/jit(take_along_axis)/gather | solution.py:43
  28.9 0.1 reshape.73
  28.9 0.1 constant_dynamic-slice_fusion.2
  29.0 0.1 copy.47
  29.1 0.0 copy-done.3
  29.1 0.1 fusion.8
  29.2 154.8 %all-reduce.3.cloned.1.call-done = (f32[32,64,64]{2,1,0:T(8,128)}, f32[2048,64]{0,1:T(8,128)}) async-done(((f32[32,64,64]{2,1,0:T(8,128)}, f32[2048,64]{0,1:T(8,128)}), (f32[32,64,64]{2,1,0:T(8,128)}, f32[2048,64]{0,1:T(8,128)})) %all-reduce.3.cloned.1.call-update) | async-done | bytes 1048592 | tf_op jit(solution)/shard_map/psum | solution.py:26
  184.0 0.8 constant_dynamic-slice_fusion.1
  184.8 0.1 reshape.57
  184.9 2.4 multiply_reduce_fusion
  187.4 0.1 reshape.59
  187.5 25.7 %psum.23 = f32[32]{0:T(128)S(1)} all-reduce(f32[32]{0:T(128)S(1)} %get-tuple-element.8), channel_id=1, replica_groups=mesh['dp'=32,'tensor'=8] {'tensor'}, use_global_device_ids=true, to_apply=%region_4.5 | all-reduce | flops 32 | bytes 256 | tf_op jit(solution)/shard_map/psum | solution.py:30
  213.2 0.1 multiply_convert_fusion
  213.2 0.6 gather_fusion
  213.9 0.5 broadcast.88
  214.4 0.7 reduce.1
  215.1 0.6 reshape.92
  215.7 9.8 %all-to-all-start = ((bf16[32,2,256]{2,1,0:T(2,128)(2,1)}), bf16[32,2,256]{2,1,0:T(2,128)(2,1)S(1)}, u32[]{:S(2)}, u32[]{:S(2)}) async-start(bf16[32,2,256]{2,1,0:T(2,128)(2,1)} %reshape.92), calls=%async_computation | async-start | bytes 65536 | tf_op jit(solution)/shard_map/all_to_all | solution.py:39
  225.5 0.0 reduce-scatter.2.cloned.1.call-start
  225.5 7.7 %all-to-all-done = bf16[32,2,256]{2,1,0:T(2,128)(2,1)S(1)} async-done(((bf16[32,2,256]{2,1,0:T(2,128)(2,1)}), bf16[32,2,256]{2,1,0:T(2,128)(2,1)S(1)}, u32[]{:S(2)}, u32[]{:S(2)}) %all-to-all-start) | async-done | bytes 32800 | tf_op jit(solution)/shard_map/all_to_all | solution.py:39
  233.2 0.7 scatter_custom_fusion
  234.0 0.0 copy-start.1
  234.0 0.0 all-gather.2.cloned.1.call-done
  234.0 2.3 convolution_multiply_fusion
  236.3 0.0 reduce-scatter.2.cloned.1.call-update
  236.3 73.0 %reduce-scatter.2.cloned.1.call-done = f32[32,128]{1,0:T(8,128)} async-done(((f32[32,1024]{1,0:T(8,128)}), f32[32,128]{1,0:T(8,128)}) %reduce-scatter.2.cloned.1.call-update) | async-done | bytes 16400 | tf_op jit(solution)/shard_map/reduce_scatter | solution.py:57
  309.3 0.0 copy-done.1
  (11 shorter events, 0.1 us)
Async XLA Ops:
  8.0 1.6 copy-start
  8.0 10.9 %copy-start.2 = (s32[1024]{0:T(1024)S(1)}, s32[1024]{0:T(1024)}, u32[]{:S(2)}) copy-start(s32[1024]{0:T(1024)} %param.12) | copy-start | bytes 12292
  8.0 176.0 %all-reduce.3.cloned.1.call-start = ((), (), s32[]{:S(2)}) async-start(), calls=%async_computation.4 | async-start | bytes 3145728 | tf_op jit(solution)/shard_map/psum | solution.py:26
  18.3 215.7 %all-gather.2.cloned.1.call-start = ((), (), s32[]{:S(2)}) async-start(), calls=%async_computation.2 | async-start | bytes 1081344 | tf_op jit(solution)/shard_map/all_gather | solution.py:52
  21.8 7.3 %copy-start.3 = (s32[32]{0:T(128)S(1)}, s32[32]{0:T(128)}, u32[]{:S(2)}) copy-start(s32[32]{0:T(128)} %param.11) | copy-start | bytes 388
  215.7 17.5 %all-to-all-start = ((bf16[32,2,256]{2,1,0:T(2,128)(2,1)}), bf16[32,2,256]{2,1,0:T(2,128)(2,1)S(1)}, u32[]{:S(2)}, u32[]{:S(2)}) async-start(bf16[32,2,256]{2,1,0:T(2,128)(2,1)} %reshape.92), calls=%async_computation | async-start | bytes 65536 | tf_op jit(solution)/shard_map/all_to_all | solution.py:39
  225.5 83.8 %reduce-scatter.2.cloned.1.call-start = ((), (), s32[]{:S(2)}) async-start(), calls=%async_computation.3 | async-start | bytes 147456 | tf_op jit(solution)/shard_map/reduce_scatter | solution.py:57
  234.0 75.3 %copy-start.1 = (bf16[32,512]{1,0:T(8,128)(2,1)}, bf16[32,512]{1,0:T(8,128)(2,1)S(1)}, u32[]{:S(2)}) copy-start(bf16[32,512]{1,0:T(8,128)(2,1)S(1)} %scatter_custom_fusion) | copy-start | bytes 98308
Sparse Core Ops, SparseCore 0:
  18.5 165.4 all-reduce.2
  236.5 72.7 reduce-scatter.1
Sparse Core Ops, SparseCore 1:
  20.7 118.1 all-gather.1
where the time goes:
time: 318 us; the launch traced here: 317 us
  waiting for transfers between devices  236 us (74%)
  blocking collectives  25.7 us (8%)
  between operations  15.6 us (5%)
  matrix products  13.4 us (4%)
  local copies, waits for them, and re-layouts  12.7 us (4%)
  starting transfers between devices  9.89 us (3%)
  other arithmetic  3.37 us (1%)
    psum x1, waiting for transfers between devices, per_device(): in_full, out_full = lax.psum((in_part, out_part), 'tensor')  155 us
    reduce_scatter x1, waiting for transfers between devices, per_device(): lax.psum_scatter(partial_scores, 'tensor', scatter_dimension=1, tiled=True)  73 us
    psum x1, blocking collectives, per_device(): squares = lax.psum(jnp.sum(kron_cols * kron_cols, axis=1), 'tensor')  25.7 us
    all_to_all x1, starting transfers between devices, per_device(): lax.all_to_all(outgoing, 'dp', split_axis=0, concat_axis=0, tiled=True)  9.77 us
    all_to_all x1, waiting for transfers between devices, per_device(): lax.all_to_all(outgoing, 'dp', split_axis=0, concat_axis=0, tiled=True)  7.67 us
    gather x4, local copies, waits for them, and re-layouts, per_device(): jnp.take_along_axis(row_table, jnp.argsort(row_table // seq_dev, axis=1,...  7.28 us
  transfers between devices with their start and end apart: 4, of which 3 were waited for; matrix products, arithmetic and copies ran while one was open for 5% of the time, Pallas kernels for 0%

commit v1 on v0

v1 whole, which is shorter than its diff:
```python
import jax
import jax.numpy as jnp
from jax import lax
from jax.experimental import pallas as pl
from jax.experimental.pallas import tpu as pltpu
from jax.sharding import PartitionSpec as P

MESH = pl.DeviceIdType.MESH
DP, TP = 32, 8
NX, NY, NZ = 4, 4, 4
SEQ, LEN, R = 32, 64, 64
STEPS = 4
CHUNKS = 8
QROWS, QCOLS = 32, 512
TOP = 32767.0


def quantize(block):
    peak = jnp.maximum(jnp.max(jnp.abs(block), axis=0, keepdims=True), 1e-30)
    values = jnp.round(block * (TOP / peak)).astype(jnp.int32).astype(jnp.int16)
    return values, peak * (1.0 / TOP)


def dequantize(values, scale):
    return values.astype(jnp.int32).astype(jnp.float32) * scale


def kernel(
    hid, grad, win, wout, lens_in, rows_in, queries, store_ref, scores_ref,
    hid_v, grad_v, win_v, wout_v, wide_in, wide_out, lens_v, rows_v, sigma_v, sigma_s,
    part, coded, scale, xsend, xsscale, xrecv, xrscale, own, zsend, zsscale, zrecv, zrscale,
    bsend, brecv, qall, flat, wide,
    load_sem, hid_sem, grad_sem, sig_sem, xs_sem, xr_sem, xcs_sem, xcr_sem,
    zs_sem, zr_sem, zcs_sem, zcr_sem, bs_sem, br_sem, qs_sem, qr_sem,
):
    dp, tn = lax.axis_index("dp"), lax.axis_index("tensor")
    zl, y, core = dp // 8, (dp // 2) % 4, dp % 2
    x, zh = tn // 2, tn % 2
    shift = dp % STEPS

    def remote(src, dst, send, recv, device):
        return pltpu.make_async_remote_copy(
            src_ref=src, dst_ref=dst, send_sem=send, recv_sem=recv, device_id=device, device_id_type=MESH
        )

    loads = [
        pltpu.make_async_copy(src, dst, load_sem.at[i])
        for i, (src, dst) in enumerate(
            [(rows_in, rows_v), (lens_in, lens_v), (win, win_v), (wout, wout_v)]
        )
    ]
    for load in loads:
        load.start()
    tokens = hid_v.shape[0] // CHUNKS
    chunk_loads = []
    for i in range(CHUNKS):
        at = pl.ds(i * tokens, tokens)
        pair = (
            pltpu.make_async_copy(hid.at[at], hid_v.at[at], hid_sem.at[i]),
            pltpu.make_async_copy(grad.at[at], grad_v.at[at], grad_sem.at[i]),
        )
        for load in pair:
            load.start()
        chunk_loads.append(pair)

    x_peers = [(dp, lax.rem(x + d, NX) * 2 + zh) for d in (1, 2, 3)]
    z_peer = (dp, x * 2 + 1 - zh)
    zl_peers = [(lax.rem(zl + d, NZ) * 8 + y * 2 + core, tn) for d in (1, 2, 3)]
    y_peers = [(zl * 8 + lax.rem(y + d, NY) * 2 + core, tn) for d in (1, 2, 3)]
    core_peer = (zl * 8 + y * 2 + 1 - core, tn)
    q_target = (x * 8 + ((y % 2) * 2 + zh) * 2 + 1 - core, zl * 2 + y // 2)
    q_source = (x * 8 + (zh * 2 + y // 2) * 2 + 1 - core, zl * 2 + y % 2)
    self_row = tn == dp // STEPS
    barrier = pltpu.get_barrier_semaphore()

    def greet(device):
        pl.semaphore_signal(barrier, inc=1, device_id=device, device_id_type=MESH)

    for device in [*x_peers, z_peer, *zl_peers, *y_peers, core_peer, q_source]:
        greet(device)
    for d in range(1, DP):
        greet((lax.rem(dp + d, DP), dp // STEPS))

    @pl.when(jnp.logical_not(self_row))
    def _():
        greet((dp, dp // STEPS))

    loads[0].wait()
    targets = lax.shift_right_logical(rows_v[pl.ds(dp, 1), :], 5)
    block_of = lax.broadcasted_iota(jnp.int32, (DP, SEQ), 0)
    seq_of = lax.broadcasted_iota(jnp.int32, (DP, SEQ), 1)
    sigma = jnp.sum(jnp.where(targets == block_of, seq_of, 0), axis=1, keepdims=True)
    sigma_v[...] = jnp.broadcast_to(jnp.minimum(sigma, SEQ - 1), sigma_v.shape)
    sig_copy = pltpu.make_async_copy(sigma_v, sigma_s, sig_sem)
    sig_copy.start()
    loads[1].wait()
    for load in loads[2:]:
        load.wait()
    zero_in = jnp.zeros_like(win_v)
    wide_in[...] = jnp.concatenate([win_v[...], zero_in], axis=1)
    zero_out = jnp.zeros_like(wout_v)
    wide_out[...] = jnp.concatenate([zero_out, wout_v[...]], axis=1)

    pl.semaphore_wait(barrier, DP + 12 - self_row.astype(jnp.int32))

    slot1 = x * 8 + ((y % 2) * 2 + zh) * 2 + 1 - core
    q_copies = [remote(queries, qall.at[slot1], qs_sem.at[0], qr_sem.at[0], q_target)]
    q_copies[0].start()

    position = lax.broadcasted_iota(jnp.int32, (LEN, 2 * R), 0)
    for i in range(CHUNKS):
        at = pl.ds(i * tokens, tokens)
        for load in chunk_loads[i]:
            load.wait()
        out = jnp.dot(hid_v[at, :], wide_in[...], preferred_element_type=jnp.float32)
        out += jnp.dot(grad_v[at, :], wide_out[...], preferred_element_type=jnp.float32)
        for j in range(tokens // LEN):
            s = i * (tokens // LEN) + j
            block = jnp.where(position < lens_v[s : s + 1, :], out[j * LEN : (j + 1) * LEN], 0.0)
            part[s] = block
            coded[s], scale[s : s + 1, :] = quantize(block)
        if i == 2:
            q_copies[0].wait_recv()
            mine = qall.at[dp]
            for d, device in enumerate(zl_peers):
                q_copies.append(remote(mine, mine, qs_sem.at[1 + d], qr_sem.at[1 + d], device))
                q_copies[-1].start()
        if i == 6:
            for copy in q_copies[1:4]:
                copy.wait_recv()
            for d, device in enumerate(y_peers):
                for z in range(NZ):
                    block = qall.at[z * 8 + y * 2 + core]
                    n = 4 + d * NZ + z
                    q_copies.append(remote(block, block, qs_sem.at[n], qr_sem.at[n], device))
                    q_copies[-1].start()

    sig_copy.wait()

    def source(k, tensor):
        return sigma_s[tensor * STEPS + lax.rem(k + shift, STEPS), 0]

    x_copies, xc_copies = {}, []
    for d in (2, 1, 3):
        for k in range(STEPS):
            for h in range(2):
                s = source(k, lax.rem(x + d, NX) * 2 + h)
                xsscale[d - 1, 2 * k + h : 2 * k + h + 1, :] = scale[pl.ds(s, 1), :]
        copy = remote(xsscale.at[d - 1], xrscale.at[d - 1], xcs_sem.at[d - 1], xcr_sem.at[d - 1], x_peers[d - 1])
        copy.start()
        xc_copies.append(copy)
    for k in range(STEPS):
        for d in (2, 1, 3):
            for h in range(2):
                xsend[d - 1, k, h] = coded[source(k, lax.rem(x + d, NX) * 2 + h)]
            n = (d - 1) * STEPS + k
            copy = remote(xsend.at[d - 1, k], xrecv.at[d - 1, k], xs_sem.at[n], xr_sem.at[n], x_peers[d - 1])
            copy.start()
            x_copies[k, d] = copy

    for copy in q_copies[4:]:
        copy.wait_recv()
    for z in range(NZ):
        for yy in range(NY):
            block = qall.at[z * 8 + yy * 2 + core]
            n = 16 + z * NY + yy
            q_copies.append(remote(block, block, qs_sem.at[n], qr_sem.at[n], core_peer))
            q_copies[-1].start()

    for copy in xc_copies:
        copy.wait_recv()
    z_copies, zc_copies, b_copies = [], [], []

    def x_sum(k, h):
        total = part[source(k, x * 2 + h)]
        for d in (1, 2, 3):
            total += dequantize(xrecv[d - 1, k, h], xrscale[d - 1, pl.ds(2 * k + h, 1), :])
        return total

    def z_step(k):
        for d in (2, 1, 3):
            x_copies[k, d].wait_recv()
        zsend[k], zsscale[k] = quantize(x_sum(k, 1 - zh))
        z_copies.append(remote(zsend.at[k], zrecv.at[k], zs_sem.at[k], zr_sem.at[k], z_peer))
        z_copies[-1].start()
        zc_copies.append(remote(zsscale.at[k], zrscale.at[k], zcs_sem.at[k], zcr_sem.at[k], z_peer))
        zc_copies[-1].start()
        own[k] = x_sum(k, zh)

    def b_step(k):
        z_copies[k].wait_recv()
        zc_copies[k].wait_recv()
        total = own[k] + dequantize(zrecv[k], zrscale[k])
        kron = lax.dot_general(
            total[:, :R], total[:, R:], (((0,), (0,)), ((), ())),
            precision=lax.Precision.HIGHEST, preferred_element_type=jnp.float32,
        )
        mean = jnp.sum(jnp.sum(kron * kron, axis=0, keepdims=True), axis=1, keepdims=True) * (1.0 / (R * R))
        normed = kron * (1.0 / jnp.sqrt(mean + 1e-06))
        bsend[k] = normed.reshape(R * R // 128, 128).astype(jnp.bfloat16)
        q = tn * STEPS + lax.rem(k + shift, STEPS)
        for d in range(TP):
            copy = remote(bsend.at[k], brecv.at[dp], bs_sem.at[k * TP + d], br_sem, (q, lax.rem(tn + d, TP)))
            if k == 0 and d == 0:

                @pl.when(self_row)
                def _():
                    pltpu.make_async_copy(bsend.at[k], brecv.at[dp], br_sem).start()

                @pl.when(jnp.logical_not(self_row))
                def _(copy=copy):
                    copy.start()
            else:
                copy.start()
            b_copies.append(copy)

    z_step(0)
    for k in range(1, STEPS):
        z_step(k)
        b_step(k - 1)
    b_step(STEPS - 1)

    rows = rows_v[...]
    slot = jnp.sum(
        jnp.where(lax.shift_right_logical(rows, 5) == dp, lax.bitwise_and(rows, 31), 0), axis=1, keepdims=True
    )
    place = lax.broadcasted_iota(jnp.int32, (DP, SEQ), 1) == slot
    for copy in q_copies[16:]:
        copy.wait_recv()

    pltpu.make_async_copy(brecv, brecv, br_sem).wait()
    flat[...] = brecv[...].reshape(flat.shape).astype(jnp.float32)
    cols = R * R // 128
    for a in range(cols):
        wide[:, a * 128 : (a + 1) * 128] = flat[pl.ds(a, DP, stride=cols), :].astype(jnp.bfloat16)
    ordered = place.astype(jnp.bfloat16)
    mine = wide[:, pl.ds(pl.multiple_of(tn * QCOLS, QCOLS), QCOLS)]
    store_ref[...] = lax.dot_general(
        ordered, mine, (((0,), (0,)), ((), ())), preferred_element_type=jnp.float32
    ).astype(jnp.bfloat16)
    total = jnp.zeros((DP, 4 * QROWS), jnp.float32)
    for c in range(TP):
        block = jnp.concatenate(
            [qall[(c // 2) * 8 + ((m // 2) * 2 + c % 2) * 2 + 1 - m % 2] for m in range(4)], axis=0
        )
        total += lax.dot_general(
            wide[:, c * QCOLS : (c + 1) * QCOLS], block, (((1,), (1,)), ((), ())), preferred_element_type=jnp.float32
        )
    scores_ref[...] = lax.dot_general(
        place.astype(jnp.float32), total, (((0,), (0,)), ((), ())),
        precision=lax.Precision.HIGHEST, preferred_element_type=jnp.float32,
    ) * (1.0 / R)

    for copy in [*q_copies, *xc_copies, *x_copies.values(), *z_copies, *zc_copies, *b_copies[1:]]:
        copy.wait_send()

    @pl.when(jnp.logical_not(self_row))
    def _():
        b_copies[0].wait_send()


def per_device(hidden_in, grad_out, proj_in, proj_out, lengths, store_row, queries):
    lens = jnp.broadcast_to(lengths[:, None], (SEQ, 2 * R))
    rows = store_row.reshape(DP, SEQ)
    dma, vmem = pltpu.SemaphoreType.DMA, pltpu.VMEM
    bf16, f32, i16, i32 = jnp.bfloat16, jnp.float32, jnp.int16, jnp.int32
    tokens, wide_k = hidden_in.shape
    narrow_k = grad_out.shape[1]
    return pl.pallas_call(
        kernel,
        out_shape=(
            jax.ShapeDtypeStruct((SEQ, QCOLS), bf16),
            jax.ShapeDtypeStruct((SEQ, 4 * QROWS), f32),
        ),
        in_specs=[pl.BlockSpec(memory_space=pl.ANY)] * 7,
        out_specs=(pl.BlockSpec(memory_space=pltpu.VMEM),) * 2,
        scratch_shapes=[
            vmem((tokens, wide_k), bf16), vmem((tokens, narrow_k), bf16),
            vmem((wide_k, R), bf16), vmem((narrow_k, R), bf16),
            vmem((wide_k, 2 * R), bf16), vmem((narrow_k, 2 * R), bf16),
            vmem((SEQ, 2 * R), i32), vmem((DP, SEQ), i32),
            vmem((DP, 128), i32), pltpu.SMEM((DP, 128), i32),
            vmem((SEQ, LEN, 2 * R), f32), vmem((SEQ, LEN, 2 * R), i16), vmem((SEQ, 2 * R), f32),
            vmem((3, STEPS, 2, LEN, 2 * R), i16), vmem((3, 2 * STEPS, 2 * R), f32),
            vmem((3, STEPS, 2, LEN, 2 * R), i16), vmem((3, 2 * STEPS, 2 * R), f32),
            vmem((STEPS, LEN, 2 * R), f32),
            vmem((STEPS, LEN, 2 * R), i16), vmem((STEPS, 1, 2 * R), f32),
            vmem((STEPS, LEN, 2 * R), i16), vmem((STEPS, 1, 2 * R), f32),
            vmem((STEPS, 32, 128), bf16), vmem((DP, 32, 128), bf16),
            vmem((DP, QROWS, QCOLS), bf16), vmem((DP * 32, 128), f32), vmem((DP, R * R), bf16),
            dma((4,)), dma((CHUNKS,)), dma((CHUNKS,)), dma,
            dma((3 * STEPS,)), dma((3 * STEPS,)), dma((3,)), dma((3,)),
            dma((STEPS,)), dma((STEPS,)), dma((STEPS,)), dma((STEPS,)),
            dma((STEPS * TP,)), dma, dma((32,)), dma((32,)),
        ],
        compiler_params=pltpu.CompilerParams(collective_id=0, has_side_effects=True, vmem_limit_bytes=48 * 2**20),
    )(hidden_in, grad_out, proj_in, proj_out, lens, rows, queries)


def solution(mesh):
    placed = (
        P("dp", "tensor"), P("dp", "tensor"), P("tensor", None), P("tensor", None),
        P("dp"), P(), P("dp", "tensor"),
    )
    return jax.shard_map(
        per_device, mesh=mesh, in_specs=placed, out_specs=(P("dp", "tensor"), P("dp", "tensor")), check_vma=False
    )
```

time: 318 us -> 60.3 us (0.19)
  the two profiles are of different devices: /device:TPU:1 before, /device:TPU:15 now
where the time goes in v1:
time: 60.3 us; the launch traced here: 60 us
  Pallas kernels  52.1 us (86%)
  local copies, waits for them, and re-layouts  7.22 us (12%)
  between operations  0.66 us (1%)
    pallas_call x1, Pallas kernels, per_device(): pl.pallas_call(kernel, out_shape=(jax.ShapeDtypeStruct((SEQ, QCOLS), bf16...  52.1 us
    unnamed x8, local copies, waits for them, and re-layouts  5.74 us

profile of v1, /device:TPU:15, one launch (start us, length us, event | category | flops | bytes accessed | tf_op | source)
XLA Modules:
  0.0 60.0 jit_solution(4903488150391335786)
XLA Ops:
  0.6 0.7 %broadcast_in_dim.2.lens_in = s32[32,128]{1,0:T(8,128)S(1)} broadcast(s32[32]{0:T(128)} %param.11), dimensions={0} | broadcast | bytes 16512 | tf_op jit(solution)/shard_map/broadcast_in_dim | solution.py:263
  1.4 0.8 %reshape.8.rows_in = s32[32,32]{1,0:T(8,128)S(1)} reshape(s32[1024]{0:T(1024)} %param.12) | data formatting | bytes 8192 | tf_op jit(solution)/shard_map/reshape | solution.py:264
  2.1 1.0 %copy.10.wout = bf16[512,64]{1,0:T(8,128)(2,1)S(1)} copy(bf16[512,64]{0,1:T(8,128)(2,1)} %param.10) | data formatting | bytes 131072 | tf_op args[3]
  3.1 1.2 %copy.9.win = bf16[1792,64]{1,0:T(8,128)(2,1)S(1)} copy(bf16[1792,64]{0,1:T(8,128)(2,1)} %param.9) | data formatting | bytes 458752 | tf_op args[2]
  4.3 0.0 copy-start
  4.3 1.6 %copy-done = bf16[2048,512]{1,0:T(8,128)(2,1)S(1)} copy-done((bf16[2048,512]{1,0:T(8,128)(2,1)S(1)}, bf16[2048,512]{1,0:T(8,128)(2,1)}, u32[]{:S(2)}) %copy-start) | copy-done | bytes 2097176
  5.9 0.0 copy-start.1
  5.9 0.8 %copy-done.1 = bf16[32,512]{1,0:T(8,128)(2,1)S(1)} copy-done((bf16[32,512]{1,0:T(8,128)(2,1)S(1)}, bf16[32,512]{1,0:T(8,128)(2,1)}, u32[]{:S(2)}) %copy-start.1) | copy-done | bytes 32792
  6.6 52.1 %shard_map.86 = (bf16[32,512]{1,0:T(8,128)(2,1)S(1)}, f32[32,128]{1,0:T(8,128)S(1)}) custom-call(bf16[2048,1792]{1,0:T(8,128)(2,1)} %hid.1, bf16[2048,512]{1,0:T(8,128)(2,1)S(1)} %copy-done, bf16[1792,64]{1,0:T(8,128)(2,1)S(1)} %copy.9.win, bf16[512,64]{1,0:T(8,128)(2,1)S(1)} %copy.10.wout, s32[32,128]{1,0:T(8,128)S(1)} %broadcast_in_dim.2.lens_in, ...), custom_call_target="tpu_custom_call" | custom-call | tf_op jit(solution)/shard_map/pallas_call | solution.py:269
  58.8 0.6 %copy.13 = bf16[32,512]{1,0:T(8,128)(2,1)} copy(bf16[32,512]{1,0:T(8,128)(2,1)S(1)} %get-tuple-element.4) | data formatting | bytes 65536
  59.4 0.6 %copy.14 = f32[32,128]{1,0:T(8,128)} copy(f32[32,128]{1,0:T(8,128)S(1)} %get-tuple-element.5) | data formatting | bytes 32768
Async XLA Ops:
  4.3 1.6 %copy-start = (bf16[2048,512]{1,0:T(8,128)(2,1)S(1)}, bf16[2048,512]{1,0:T(8,128)(2,1)}, u32[]{:S(2)}) copy-start(bf16[2048,512]{1,0:T(8,128)(2,1)} %grad.1) | copy-start | bytes 6291460
  5.9 0.8 %copy-start.1 = (bf16[32,512]{1,0:T(8,128)(2,1)S(1)}, bf16[32,512]{1,0:T(8,128)(2,1)}, u32[]{:S(2)}) copy-start(bf16[32,512]{1,0:T(8,128)(2,1)} %queries.1) | copy-start | bytes 98308

commit v2 on v1

--- a/solution.py
+++ b/solution.py
@@ -11,6 +11,8 @@
 SEQ, LEN, R = 32, 64, 64
 STEPS = 4
 CHUNKS = 8
+AHEAD = 3
+GREET = 3
 QROWS, QCOLS = 32, 512
 TOP = 32767.0
 
@@ -27,11 +29,11 @@
 
 def kernel(
     hid, grad, win, wout, lens_in, rows_in, queries, store_ref, scores_ref,
-    hid_v, grad_v, win_v, wout_v, wide_in, wide_out, lens_v, rows_v, sigma_v, sigma_s,
+    hid_v, grad_v, win_v, wout_v, wide_in, wide_out, lens_s, rows_v, sigma_v, sigma_s,
     part, coded, scale, xsend, xsscale, xrecv, xrscale, own, zsend, zsscale, zrecv, zrscale,
     bsend, brecv, qall, flat, wide,
     load_sem, hid_sem, grad_sem, sig_sem, xs_sem, xr_sem, xcs_sem, xcr_sem,
-    zs_sem, zr_sem, zcs_sem, zcr_sem, bs_sem, br_sem, qs_sem, qr_sem,
+    zs_sem, zr_sem, zcs_sem, zcr_sem, bs_sem, br_sem, qs_sem, qr_sem, known_sem,
 ):
     dp, tn = lax.axis_index("dp"), lax.axis_index("tensor")
     zl, y, core = dp // 8, (dp // 2) % 4, dp % 2
@@ -46,7 +48,7 @@
     loads = [
         pltpu.make_async_copy(src, dst, load_sem.at[i])
         for i, (src, dst) in enumerate(
-            [(rows_in, rows_v), (lens_in, lens_v), (win, win_v), (wout, wout_v)]
+            [(rows_in, rows_v), (lens_in, lens_s), (win, win_v), (wout, wout_v)]
         )
     ]
     for load in loads:
@@ -55,85 +57,71 @@
     chunk_loads = []
     for i in range(CHUNKS):
         at = pl.ds(i * tokens, tokens)
-        pair = (
+        chunk_loads.append((
             pltpu.make_async_copy(hid.at[at], hid_v.at[at], hid_sem.at[i]),
             pltpu.make_async_copy(grad.at[at], grad_v.at[at], grad_sem.at[i]),
-        )
+        ))
+    for pair in chunk_loads[:AHEAD]:
         for load in pair:
             load.start()
-        chunk_loads.append(pair)
 
     x_peers = [(dp, lax.rem(x + d, NX) * 2 + zh) for d in (1, 2, 3)]
     z_peer = (dp, x * 2 + 1 - zh)
-    zl_peers = [(lax.rem(zl + d, NZ) * 8 + y * 2 + core, tn) for d in (1, 2, 3)]
     y_peers = [(zl * 8 + lax.rem(y + d, NY) * 2 + core, tn) for d in (1, 2, 3)]
     core_peer = (zl * 8 + y * 2 + 1 - core, tn)
-    q_target = (x * 8 + ((y % 2) * 2 + zh) * 2 + 1 - core, zl * 2 + y // 2)
-    q_source = (x * 8 + (zh * 2 + y // 2) * 2 + 1 - core, zl * 2 + y % 2)
+    q_y = (y % 2) * 2 + zh
+    q_targets = [(z * 8 + q_y * 2 + 1 - core, zl * 2 + y // 2) for z in range(NZ)]
+    q_sources = [(x * 8 + (zh * 2 + y // 2) * 2 + 1 - core, z * 2 + y % 2) for z in range(NX)]
     self_row = tn == dp // STEPS
     barrier = pltpu.get_barrier_semaphore()
 
-    def greet(device):
-        pl.semaphore_signal(barrier, inc=1, device_id=device, device_id_type=MESH)
-
-    for device in [*x_peers, z_peer, *zl_peers, *y_peers, core_peer, q_source]:
-        greet(device)
-    for d in range(1, DP):
-        greet((lax.rem(dp + d, DP), dp // STEPS))
-
-    @pl.when(jnp.logical_not(self_row))
-    def _():
-        greet((dp, dp // STEPS))
+    def signal(sem, devices):
+        for device in devices:
+            pl.semaphore_signal(sem, inc=1, device_id=device, device_id_type=MESH)
+
+    signal(barrier, [*q_sources, z_peer, *x_peers, *y_peers, core_peer])
 
     loads[0].wait()
-    targets = lax.shift_right_logical(rows_v[pl.ds(dp, 1), :], 5)
-    block_of = lax.broadcasted_iota(jnp.int32, (DP, SEQ), 0)
-    seq_of = lax.broadcasted_iota(jnp.int32, (DP, SEQ), 1)
-    sigma = jnp.sum(jnp.where(targets == block_of, seq_of, 0), axis=1, keepdims=True)
+    rows = rows_v[...]
+    flat_at = lax.broadcasted_iota(jnp.int32, rows.shape, 0) * 128 + lax.broadcasted_iota(jnp.int32, rows.shape, 1)
+    holder, seq_of = lax.shift_right_logical(flat_at, 5), lax.bitwise_and(flat_at, 31)
+    block_of, place_of = lax.shift_right_logical(rows, 5), lax.bitwise_and(rows, 31)
+    block_of = jnp.where(holder == dp, block_of, -1)
+    each = lax.broadcasted_iota(jnp.int32, (DP, *rows.shape), 0)
+    sigma = jnp.sum(jnp.where(block_of[None] == each, seq_of[None], 0), axis=1)
+    sigma = jnp.sum(sigma, axis=1, keepdims=True)
     sigma_v[...] = jnp.broadcast_to(jnp.minimum(sigma, SEQ - 1), sigma_v.shape)
     sig_copy = pltpu.make_async_copy(sigma_v, sigma_s, sig_sem)
     sig_copy.start()
     loads[1].wait()
     for load in loads[2:]:
         load.wait()
-    zero_in = jnp.zeros_like(win_v)
-    wide_in[...] = jnp.concatenate([win_v[...], zero_in], axis=1)
-    zero_out = jnp.zeros_like(wout_v)
-    wide_out[...] = jnp.concatenate([zero_out, wout_v[...]], axis=1)
-
-    pl.semaphore_wait(barrier, DP + 12 - self_row.astype(jnp.int32))
-
-    slot1 = x * 8 + ((y % 2) * 2 + zh) * 2 + 1 - core
-    q_copies = [remote(queries, qall.at[slot1], qs_sem.at[0], qr_sem.at[0], q_target)]
-    q_copies[0].start()
-
+    wide_in[...] = jnp.concatenate([win_v[...], jnp.zeros_like(win_v)], axis=0).T
+    wide_out[...] = jnp.concatenate([jnp.zeros_like(wout_v), wout_v[...]], axis=0).T
+
+    q_copies = []
     position = lax.broadcasted_iota(jnp.int32, (LEN, 2 * R), 0)
     for i in range(CHUNKS):
         at = pl.ds(i * tokens, tokens)
         for load in chunk_loads[i]:
             load.wait()
+        if i + AHEAD < CHUNKS:
+            for load in chunk_loads[i + AHEAD]:
+                load.start()
         out = jnp.dot(hid_v[at, :], wide_in[...], preferred_element_type=jnp.float32)
         out += jnp.dot(grad_v[at, :], wide_out[...], preferred_element_type=jnp.float32)
         for j in range(tokens // LEN):
             s = i * (tokens // LEN) + j
-            block = jnp.where(position < lens_v[s : s + 1, :], out[j * LEN : (j + 1) * LEN], 0.0)
+            block = jnp.where(position < lens_s[s], out[j * LEN : (j + 1) * LEN], 0.0)
             part[s] = block
             coded[s], scale[s : s + 1, :] = quantize(block)
-        if i == 2:
-            q_copies[0].wait_recv()
-            mine = qall.at[dp]
-            for d, device in enumerate(zl_peers):
-                q_copies.append(remote(mine, mine, qs_sem.at[1 + d], qr_sem.at[1 + d], device))
+        if i == GREET:
+            pl.semaphore_wait(barrier, 12)
+            for z, device in enumerate(q_targets):
+                q_copies.append(
+                    remote(queries, qall.at[1 - core, q_y, x], qs_sem.at[z], qr_sem.at[x], device)
+                )
                 q_copies[-1].start()
-        if i == 6:
-            for copy in q_copies[1:4]:
-                copy.wait_recv()
-            for d, device in enumerate(y_peers):
-                for z in range(NZ):
-                    block = qall.at[z * 8 + y * 2 + core]
-                    n = 4 + d * NZ + z
-                    q_copies.append(remote(block, block, qs_sem.at[n], qr_sem.at[n], device))
-                    q_copies[-1].start()
 
     sig_copy.wait()
 
@@ -158,15 +146,6 @@
             copy.start()
             x_copies[k, d] = copy
 
-    for copy in q_copies[4:]:
-        copy.wait_recv()
-    for z in range(NZ):
-        for yy in range(NY):
-            block = qall.at[z * 8 + yy * 2 + core]
-            n = 16 + z * NY + yy
-            q_copies.append(remote(block, block, qs_sem.at[n], qr_sem.at[n], core_peer))
-            q_copies[-1].start()
-
     for copy in xc_copies:
         copy.wait_recv()
     z_copies, zc_copies, b_copies = [], [], []
@@ -215,18 +194,32 @@
             b_copies.append(copy)
 
     z_step(0)
-    for k in range(1, STEPS):
-        z_step(k)
-        b_step(k - 1)
-    b_step(STEPS - 1)
-
-    rows = rows_v[...]
-    slot = jnp.sum(
-        jnp.where(lax.shift_right_logical(rows, 5) == dp, lax.bitwise_and(rows, 31), 0), axis=1, keepdims=True
-    )
+    z_step(1)
+    mine = qall.at[core, y]
+    for i in range(NX):
+        pltpu.make_async_copy(queries, mine.at[i], qr_sem.at[i]).wait()
+    for d, device in enumerate(y_peers):
+        q_copies.append(remote(mine, mine, qs_sem.at[4 + d], qr_sem.at[4 + d], device))
+        q_copies[-1].start()
+    signal(known_sem.at[0], y_peers)
+    z_step(2)
+    z_step(3)
+    pl.semaphore_wait(known_sem.at[0], 3)
+    signal(known_sem.at[1], [core_peer])
+    pl.semaphore_wait(known_sem.at[1], 1)
+    for k in range(STEPS):
+        b_step(k)
+    for copy in q_copies[4:]:
+        copy.wait_recv()
+    mine = qall.at[core]
+    q_copies.append(remote(mine, mine, qs_sem.at[7], qr_sem.at[7], core_peer))
+    q_copies[-1].start()
+
+    stored_here = jnp.where(lax.shift_right_logical(rows, 5) == dp, place_of, 0)
+    slot = jnp.sum(jnp.where(holder[None] == each, stored_here[None], 0), axis=1)
+    slot = jnp.sum(slot, axis=1, keepdims=True)
     place = lax.broadcasted_iota(jnp.int32, (DP, SEQ), 1) == slot
-    for copy in q_copies[16:]:
-        copy.wait_recv()
+    q_copies[-1].wait_recv()
 
     pltpu.make_async_copy(brecv, brecv, br_sem).wait()
     flat[...] = brecv[...].reshape(flat.shape).astype(jnp.float32)
@@ -241,7 +234,7 @@
     total = jnp.zeros((DP, 4 * QROWS), jnp.float32)
     for c in range(TP):
         block = jnp.concatenate(
-            [qall[(c // 2) * 8 + ((m // 2) * 2 + c % 2) * 2 + 1 - m % 2] for m in range(4)], axis=0
+            [qall[1 - m % 2, (m // 2) * 2 + c % 2, c // 2] for m in range(4)], axis=0
         )
         total += lax.dot_general(
             wide[:, c * QCOLS : (c + 1) * QCOLS], block, (((1,), (1,)), ((), ())), preferred_element_type=jnp.float32
@@ -260,8 +253,7 @@
 
 
 def per_device(hidden_in, grad_out, proj_in, proj_out, lengths, store_row, queries):
-    lens = jnp.broadcast_to(lengths[:, None], (SEQ, 2 * R))
-    rows = store_row.reshape(DP, SEQ)
+    rows = store_row.reshape(-1, 128)
     dma, vmem = pltpu.SemaphoreType.DMA, pltpu.VMEM
     bf16, f32, i16, i32 = jnp.bfloat16, jnp.float32, jnp.int16, jnp.int32
     tokens, wide_k = hidden_in.shape
@@ -272,13 +264,13 @@
             jax.ShapeDtypeStruct((SEQ, QCOLS), bf16),
             jax.ShapeDtypeStruct((SEQ, 4 * QROWS), f32),
         ),
-        in_specs=[pl.BlockSpec(memory_space=pl.ANY)] * 7,
+        in_specs=[pl.BlockSpec(memory_space=pltpu.HBM)] * 7,
         out_specs=(pl.BlockSpec(memory_space=pltpu.VMEM),) * 2,
         scratch_shapes=[
             vmem((tokens, wide_k), bf16), vmem((tokens, narrow_k), bf16),
-            vmem((wide_k, R), bf16), vmem((narrow_k, R), bf16),
+            vmem((R, wide_k), bf16), vmem((R, narrow_k), bf16),
             vmem((wide_k, 2 * R), bf16), vmem((narrow_k, 2 * R), bf16),
-            vmem((SEQ, 2 * R), i32), vmem((DP, SEQ), i32),
+            pltpu.SMEM((SEQ,), i32), vmem(rows.shape, i32),
             vmem((DP, 128), i32), pltpu.SMEM((DP, 128), i32),
             vmem((SEQ, LEN, 2 * R), f32), vmem((SEQ, LEN, 2 * R), i16), vmem((SEQ, 2 * R), f32),
             vmem((3, STEPS, 2, LEN, 2 * R), i16), vmem((3, 2 * STEPS, 2 * R), f32),
@@ -287,14 +279,14 @@
             vmem((STEPS, LEN, 2 * R), i16), vmem((STEPS, 1, 2 * R), f32),
             vmem((STEPS, LEN, 2 * R), i16), vmem((STEPS, 1, 2 * R), f32),
             vmem((STEPS, 32, 128), bf16), vmem((DP, 32, 128), bf16),
-            vmem((DP, QROWS, QCOLS), bf16), vmem((DP * 32, 128), f32), vmem((DP, R * R), bf16),
+            vmem((2, NY, NX, QROWS, QCOLS), bf16), vmem((DP * 32, 128), f32), vmem((DP, R * R), bf16),
             dma((4,)), dma((CHUNKS,)), dma((CHUNKS,)), dma,
             dma((3 * STEPS,)), dma((3 * STEPS,)), dma((3,)), dma((3,)),
             dma((STEPS,)), dma((STEPS,)), dma((STEPS,)), dma((STEPS,)),
-            dma((STEPS * TP,)), dma, dma((32,)), dma((32,)),
+            dma((STEPS * TP,)), dma, dma((8,)), dma((8,)), pltpu.SemaphoreType.REGULAR((2,)),
         ],
-        compiler_params=pltpu.CompilerParams(collective_id=0, has_side_effects=True, vmem_limit_bytes=48 * 2**20),
-    )(hidden_in, grad_out, proj_in, proj_out, lens, rows, queries)
+        compiler_params=pltpu.CompilerParams(collective_id=0, has_side_effects=True, vmem_limit_bytes=63 * 2**20),
+    )(hidden_in, grad_out, proj_in.T, proj_out.T, lengths, rows, queries)
 
 
 def solution(mesh):

time: 60.3 us -> 44.6 us (0.74)
  the two profiles are of different devices: /device:TPU:15 before, /device:TPU:17 now
where the time goes in v2:
time: 44.6 us; the launch traced here: 44.4 us
  Pallas kernels  41 us (92%)
  local copies, waits for them, and re-layouts  2.7 us (6%)
  between operations  0.64 us (1%)
    pallas_call x1, Pallas kernels, per_device(): pl.pallas_call(kernel, out_shape=(jax.ShapeDtypeStruct((SEQ, QCOLS), bf16...  41 us
    unnamed x2, local copies, waits for them, and re-layouts  2.7 us

profile of v2, /device:TPU:17, one launch (start us, length us, event | category | flops | bytes accessed | tf_op | source)
XLA Modules:
  0.0 44.4 jit_solution(7359243502530875946)
XLA Ops:
  0.6 41.0 %shard_map.86 = (bf16[32,512]{1,0:T(8,128)(2,1)}, f32[32,128]{1,0:T(8,128)}) custom-call(bf16[2048,1792]{1,0:T(8,128)(2,1)} %hid.1, bf16[2048,512]{1,0:T(8,128)(2,1)} %grad.1, bf16[64,1792]{1,0:T(8,128)(2,1)} %bitcast.3, bf16[64,512]{1,0:T(8,128)(2,1)} %bitcast.4, s32[32]{0:T(128)} %lens_in.1, s32[8,128]{1,0:T(8,128)} %bitcast.5, bf16[32,512]{1,0:T(8,128)(2,1)} %queries.1), custom_call_target="tpu_custom_call" | custom-call | tf_op jit(solution)/shard_map/pallas_call | solution.py:261
  41.7 1.4 %copy.11 = bf16[32,512]{1,0:T(8,128)(2,1)} copy(bf16[32,512]{1,0:T(8,128)(2,1)} %get-tuple-element.4) | data formatting | bytes 65536
  43.0 1.3 %copy.12 = f32[32,128]{1,0:T(8,128)} copy(f32[32,128]{1,0:T(8,128)} %get-tuple-element.5) | data formatting | bytes 32768

commit v3 on v2

--- a/solution.py
+++ b/solution.py
@@ -11,8 +11,8 @@
 SEQ, LEN, R = 32, 64, 64
 STEPS = 4
 CHUNKS = 8
-AHEAD = 3
-GREET = 3
+AHEAD = 4
+GREET = 1
 QROWS, QCOLS = 32, 512
 TOP = 32767.0
 
@@ -27,10 +27,32 @@
     return values.astype(jnp.int32).astype(jnp.float32) * scale
 
 
+def crossed(a, b):
+    return ((a - b == 3) | (b - a == 3)).astype(jnp.int32)
+
+
+def tables(rows):
+    at = lax.broadcasted_iota(jnp.int32, rows.shape, 0) * 128 + lax.broadcasted_iota(jnp.int32, rows.shape, 1)
+    high, low = lambda v: lax.shift_right_logical(v, 5), lambda v: lax.bitwise_and(v, 31)
+    return high(at), low(at), high(rows), low(rows)
+
+
+def pick(keys, values, mask):
+    keys = jnp.where(mask, keys, -1)
+    each = lax.broadcasted_iota(jnp.int32, (DP, *keys.shape), 0)
+    found = jnp.sum(jnp.where(keys[None] == each, values[None], 0), axis=1)
+    return jnp.sum(found, axis=1, keepdims=True)
+
+
+def own_order(rows, dp):
+    holder, number, block, _ = tables(rows)
+    return jnp.minimum(pick(block, number, holder == dp), SEQ - 1)
+
+
 def kernel(
     hid, grad, win, wout, lens_in, rows_in, queries, store_ref, scores_ref,
     hid_v, grad_v, win_v, wout_v, wide_in, wide_out, lens_s, rows_v, sigma_v, sigma_s,
-    part, coded, scale, xsend, xsscale, xrecv, xrscale, own, zsend, zsscale, zrecv, zrscale,
+    part, coded, scale, xsend, xsscale, xrecv, xrscale, zsend, zsscale, zrecv, zrscale,
     bsend, brecv, qall, flat, wide,
     load_sem, hid_sem, grad_sem, sig_sem, xs_sem, xr_sem, xcs_sem, xcr_sem,
     zs_sem, zr_sem, zcs_sem, zcr_sem, bs_sem, br_sem, qs_sem, qr_sem, known_sem,
@@ -38,7 +60,6 @@
     dp, tn = lax.axis_index("dp"), lax.axis_index("tensor")
     zl, y, core = dp // 8, (dp // 2) % 4, dp % 2
     x, zh = tn // 2, tn % 2
-    shift = dp % STEPS
 
     def remote(src, dst, send, recv, device):
         return pltpu.make_async_remote_copy(
@@ -61,9 +82,9 @@
             pltpu.make_async_copy(hid.at[at], hid_v.at[at], hid_sem.at[i]),
             pltpu.make_async_copy(grad.at[at], grad_v.at[at], grad_sem.at[i]),
         ))
-    for pair in chunk_loads[:AHEAD]:
+    for i, pair in enumerate(chunk_loads[:AHEAD]):
         for load in pair:
-            load.start()
+            load.start(priority=int(i > 0))
 
     x_peers = [(dp, lax.rem(x + d, NX) * 2 + zh) for d in (1, 2, 3)]
     z_peer = (dp, x * 2 + 1 - zh)
@@ -72,27 +93,24 @@
     q_y = (y % 2) * 2 + zh
     q_targets = [(z * 8 + q_y * 2 + 1 - core, zl * 2 + y // 2) for z in range(NZ)]
     q_sources = [(x * 8 + (zh * 2 + y // 2) * 2 + 1 - core, z * 2 + y % 2) for z in range(NX)]
-    self_row = tn == dp // STEPS
+    row_sources = [(z * 8 + x * 2 + core, zl * 2 + (zh + crossed(z, zl)) % 2) for z in range(NZ)]
+    row_zh = (zh + crossed(zl, x)) % 2
+    self_row = x == zl
     barrier = pltpu.get_barrier_semaphore()
 
     def signal(sem, devices):
         for device in devices:
             pl.semaphore_signal(sem, inc=1, device_id=device, device_id_type=MESH)
 
+    own_source = (x == zl) & (x == y)
     signal(barrier, [*q_sources, z_peer, *x_peers, *y_peers, core_peer])
-
-    loads[0].wait()
-    rows = rows_v[...]
-    flat_at = lax.broadcasted_iota(jnp.int32, rows.shape, 0) * 128 + lax.broadcasted_iota(jnp.int32, rows.shape, 1)
-    holder, seq_of = lax.shift_right_logical(flat_at, 5), lax.bitwise_and(flat_at, 31)
-    block_of, place_of = lax.shift_right_logical(rows, 5), lax.bitwise_and(rows, 31)
-    block_of = jnp.where(holder == dp, block_of, -1)
-    each = lax.broadcasted_iota(jnp.int32, (DP, *rows.shape), 0)
-    sigma = jnp.sum(jnp.where(block_of[None] == each, seq_of[None], 0), axis=1)
-    sigma = jnp.sum(sigma, axis=1, keepdims=True)
-    sigma_v[...] = jnp.broadcast_to(jnp.minimum(sigma, SEQ - 1), sigma_v.shape)
+    for z, device in enumerate(row_sources):
+
+        @pl.when(jnp.logical_not(own_source & (z == zl)))
+        def _(device=device):
+            signal(barrier, [device])
+
     sig_copy = pltpu.make_async_copy(sigma_v, sigma_s, sig_sem)
-    sig_copy.start()
     loads[1].wait()
     for load in loads[2:]:
         load.wait()
@@ -107,7 +125,7 @@
             load.wait()
         if i + AHEAD < CHUNKS:
             for load in chunk_loads[i + AHEAD]:
-                load.start()
+                load.start(priority=1)
         out = jnp.dot(hid_v[at, :], wide_in[...], preferred_element_type=jnp.float32)
         out += jnp.dot(grad_v[at, :], wide_out[...], preferred_element_type=jnp.float32)
         for j in range(tokens // LEN):
@@ -115,8 +133,13 @@
             block = jnp.where(position < lens_s[s], out[j * LEN : (j + 1) * LEN], 0.0)
             part[s] = block
             coded[s], scale[s : s + 1, :] = quantize(block)
+        if i == 2:
+            loads[0].wait()
+            sigma_v[...] = jnp.broadcast_to(own_order(rows_v[...], dp), sigma_v.shape)
+            sig_copy.start()
         if i == GREET:
-            pl.semaphore_wait(barrier, 12)
+            pl.semaphore_wait(barrier, 16 - own_source.astype(jnp.int32))
+            signal(known_sem.at[0], y_peers)
             for z, device in enumerate(q_targets):
                 q_copies.append(
                     remote(queries, qall.at[1 - core, q_y, x], qs_sem.at[z], qr_sem.at[x], device)
@@ -125,14 +148,17 @@
 
     sig_copy.wait()
 
-    def source(k, tensor):
-        return sigma_s[tensor * STEPS + lax.rem(k + shift, STEPS), 0]
+    def store_block(xx, k, h):
+        return xx * 8 + lax.rem(2 * k + h + dp, 8)
+
+    def source(xx, k, h):
+        return sigma_s[store_block(xx, k, h), 0]
 
     x_copies, xc_copies = {}, []
     for d in (2, 1, 3):
         for k in range(STEPS):
             for h in range(2):
-                s = source(k, lax.rem(x + d, NX) * 2 + h)
+                s = source(lax.rem(x + d, NX), k, h)
                 xsscale[d - 1, 2 * k + h : 2 * k + h + 1, :] = scale[pl.ds(s, 1), :]
         copy = remote(xsscale.at[d - 1], xrscale.at[d - 1], xcs_sem.at[d - 1], xcr_sem.at[d - 1], x_peers[d - 1])
         copy.start()
@@ -140,7 +166,7 @@
     for k in range(STEPS):
         for d in (2, 1, 3):
             for h in range(2):
-                xsend[d - 1, k, h] = coded[source(k, lax.rem(x + d, NX) * 2 + h)]
+                xsend[d - 1, k, h] = coded[source(lax.rem(x + d, NX), k, h)]
             n = (d - 1) * STEPS + k
             copy = remote(xsend.at[d - 1, k], xrecv.at[d - 1, k], xs_sem.at[n], xr_sem.at[n], x_peers[d - 1])
             copy.start()
@@ -150,62 +176,67 @@
         copy.wait_recv()
     z_copies, zc_copies, b_copies = [], [], []
 
-    def x_sum(k, h):
-        total = part[source(k, x * 2 + h)]
-        for d in (1, 2, 3):
-            total += dequantize(xrecv[d - 1, k, h], xrscale[d - 1, pl.ds(2 * k + h, 1), :])
-        return total
-
     def z_step(k):
         for d in (2, 1, 3):
             x_copies[k, d].wait_recv()
-        zsend[k], zsscale[k] = quantize(x_sum(k, 1 - zh))
+        for h in range(2):
+            total = part[source(x, k, h)]
+            for d in (1, 2, 3):
+                n = 2 * k + h
+                total += dequantize(xrecv[d - 1, k, h], xrscale[d - 1, n : n + 1, :])
+            zsend[k, h], zsscale[k, h : h + 1, :] = quantize(total)
         z_copies.append(remote(zsend.at[k], zrecv.at[k], zs_sem.at[k], zr_sem.at[k], z_peer))
         z_copies[-1].start()
         zc_copies.append(remote(zsscale.at[k], zrscale.at[k], zcs_sem.at[k], zcr_sem.at[k], z_peer))
         zc_copies[-1].start()
-        own[k] = x_sum(k, zh)
 
     def b_step(k):
         z_copies[k].wait_recv()
         zc_copies[k].wait_recv()
-        total = own[k] + dequantize(zrecv[k], zrscale[k])
-        kron = lax.dot_general(
-            total[:, :R], total[:, R:], (((0,), (0,)), ((), ())),
-            precision=lax.Precision.HIGHEST, preferred_element_type=jnp.float32,
-        )
-        mean = jnp.sum(jnp.sum(kron * kron, axis=0, keepdims=True), axis=1, keepdims=True) * (1.0 / (R * R))
-        normed = kron * (1.0 / jnp.sqrt(mean + 1e-06))
-        bsend[k] = normed.reshape(R * R // 128, 128).astype(jnp.bfloat16)
-        q = tn * STEPS + lax.rem(k + shift, STEPS)
-        for d in range(TP):
-            copy = remote(bsend.at[k], brecv.at[dp], bs_sem.at[k * TP + d], br_sem, (q, lax.rem(tn + d, TP)))
-            if k == 0 and d == 0:
-
-                @pl.when(self_row)
-                def _():
-                    pltpu.make_async_copy(bsend.at[k], brecv.at[dp], br_sem).start()
-
-                @pl.when(jnp.logical_not(self_row))
-                def _(copy=copy):
+        for h in range(2):
+            total = dequantize(zsend[k, h], zsscale[k, h : h + 1, :])
+            total += dequantize(zrecv[k, h], zrscale[k, h : h + 1, :])
+            kron = lax.dot_general(
+                total[:, :R], total[:, R:], (((0,), (0,)), ((), ())),
+                precision=lax.Precision.HIGHEST, preferred_element_type=jnp.float32,
+            )
+            mean = jnp.sum(jnp.sum(kron * kron, axis=0, keepdims=True), axis=1, keepdims=True) * (1.0 / (R * R))
+            normed = kron * (1.0 / jnp.sqrt(mean + 1e-06))
+            bsend[2 * k + h] = normed.reshape(R * R // 128, 128).astype(jnp.bfloat16)
+        for h in range(2):
+            q = store_block(x, k, h)
+            row = bsend.at[2 * k + h]
+            for d in (2, 1, 3, 0):
+                n = (2 * k + h) * NX + d
+                copy = remote(row, brecv.at[dp], bs_sem.at[n], br_sem, (q, lax.rem(x + d, NX) * 2 + row_zh))
+                if k == 0 and h == 0 and d == 0:
+
+                    @pl.when(self_row)
+                    def _(row=row):
+                        pltpu.make_async_copy(row, brecv.at[dp], br_sem).start()
+
+                    @pl.when(jnp.logical_not(self_row))
+                    def _(copy=copy):
+                        copy.start()
+
+                    first_copy.append(copy)
+                else:
                     copy.start()
-            else:
-                copy.start()
-            b_copies.append(copy)
-
+                    b_copies.append(copy)
+
+    first_copy = []
     z_step(0)
-    z_step(1)
     mine = qall.at[core, y]
     for i in range(NX):
         pltpu.make_async_copy(queries, mine.at[i], qr_sem.at[i]).wait()
     for d, device in enumerate(y_peers):
         q_copies.append(remote(mine, mine, qs_sem.at[4 + d], qr_sem.at[4 + d], device))
         q_copies[-1].start()
-    signal(known_sem.at[0], y_peers)
+    z_step(1)
+    pl.semaphore_wait(known_sem.at[0], 3)
+    signal(known_sem.at[1], [core_peer])
     z_step(2)
     z_step(3)
-    pl.semaphore_wait(known_sem.at[0], 3)
-    signal(known_sem.at[1], [core_peer])
     pl.semaphore_wait(known_sem.at[1], 1)
     for k in range(STEPS):
         b_step(k)
@@ -215,9 +246,8 @@
     q_copies.append(remote(mine, mine, qs_sem.at[7], qr_sem.at[7], core_peer))
     q_copies[-1].start()
 
-    stored_here = jnp.where(lax.shift_right_logical(rows, 5) == dp, place_of, 0)
-    slot = jnp.sum(jnp.where(holder[None] == each, stored_here[None], 0), axis=1)
-    slot = jnp.sum(slot, axis=1, keepdims=True)
+    holder, _, block, row = tables(rows_v[...])
+    slot = pick(holder, row, block == dp)
     place = lax.broadcasted_iota(jnp.int32, (DP, SEQ), 1) == slot
     q_copies[-1].wait_recv()
 
@@ -244,12 +274,12 @@
         precision=lax.Precision.HIGHEST, preferred_element_type=jnp.float32,
     ) * (1.0 / R)
 
-    for copy in [*q_copies, *xc_copies, *x_copies.values(), *z_copies, *zc_copies, *b_copies[1:]]:
+    for copy in [*q_copies, *xc_copies, *x_copies.values(), *z_copies, *zc_copies, *b_copies]:
         copy.wait_send()
 
     @pl.when(jnp.logical_not(self_row))
     def _():
-        b_copies[0].wait_send()
+        first_copy[0].wait_send()
 
 
 def per_device(hidden_in, grad_out, proj_in, proj_out, lengths, store_row, queries):
@@ -275,15 +305,14 @@
             vmem((SEQ, LEN, 2 * R), f32), vmem((SEQ, LEN, 2 * R), i16), vmem((SEQ, 2 * R), f32),
             vmem((3, STEPS, 2, LEN, 2 * R), i16), vmem((3, 2 * STEPS, 2 * R), f32),
             vmem((3, STEPS, 2, LEN, 2 * R), i16), vmem((3, 2 * STEPS, 2 * R), f32),
-            vmem((STEPS, LEN, 2 * R), f32),
-            vmem((STEPS, LEN, 2 * R), i16), vmem((STEPS, 1, 2 * R), f32),
-            vmem((STEPS, LEN, 2 * R), i16), vmem((STEPS, 1, 2 * R), f32),
-            vmem((STEPS, 32, 128), bf16), vmem((DP, 32, 128), bf16),
+            vmem((STEPS, 2, LEN, 2 * R), i16), vmem((STEPS, 2, 2 * R), f32),
+            vmem((STEPS, 2, LEN, 2 * R), i16), vmem((STEPS, 2, 2 * R), f32),
+            vmem((2 * STEPS, 32, 128), bf16), vmem((DP, 32, 128), bf16),
             vmem((2, NY, NX, QROWS, QCOLS), bf16), vmem((DP * 32, 128), f32), vmem((DP, R * R), bf16),
             dma((4,)), dma((CHUNKS,)), dma((CHUNKS,)), dma,
             dma((3 * STEPS,)), dma((3 * STEPS,)), dma((3,)), dma((3,)),
             dma((STEPS,)), dma((STEPS,)), dma((STEPS,)), dma((STEPS,)),
-            dma((STEPS * TP,)), dma, dma((8,)), dma((8,)), pltpu.SemaphoreType.REGULAR((2,)),
+            dma((2 * STEPS * NX,)), dma, dma((8,)), dma((8,)), pltpu.SemaphoreType.REGULAR((2,)),
         ],
         compiler_params=pltpu.CompilerParams(collective_id=0, has_side_effects=True, vmem_limit_bytes=63 * 2**20),
     )(hidden_in, grad_out, proj_in.T, proj_out.T, lengths, rows, queries)

time: 44.6 us -> 45.2 us (1.013)
  the two profiles are of different devices: /device:TPU:17 before, /device:TPU:1 now
where the time goes in v3:
time: 45.2 us; the launch traced here: 45 us
  Pallas kernels  41.6 us (92%)
  local copies, waits for them, and re-layouts  2.7 us (6%)
  between operations  0.64 us (1%)
    pallas_call x1, Pallas kernels, per_device(): pl.pallas_call(kernel, out_shape=(jax.ShapeDtypeStruct((SEQ, QCOLS), bf16...  41.6 us
    unnamed x2, local copies, waits for them, and re-layouts  2.7 us

profile of v3, /device:TPU:1, one launch (start us, length us, event | category | flops | bytes accessed | tf_op | source)
XLA Modules:
  0.0 45.0 jit_solution(8912924227258249073)
XLA Ops:
  0.6 41.6 %shard_map.86 = (bf16[32,512]{1,0:T(8,128)(2,1)}, f32[32,128]{1,0:T(8,128)}) custom-call(bf16[2048,1792]{1,0:T(8,128)(2,1)} %hid.1, bf16[2048,512]{1,0:T(8,128)(2,1)} %grad.1, bf16[64,1792]{1,0:T(8,128)(2,1)} %bitcast.3, bf16[64,512]{1,0:T(8,128)(2,1)} %bitcast.4, s32[32]{0:T(128)} %lens_in.1, s32[8,128]{1,0:T(8,128)} %bitcast.5, bf16[32,512]{1,0:T(8,128)(2,1)} %queries.1), custom_call_target="tpu_custom_call" | custom-call | tf_op jit(solution)/shard_map/pallas_call | solution.py:291
  42.3 1.4 %copy.11 = bf16[32,512]{1,0:T(8,128)(2,1)} copy(bf16[32,512]{1,0:T(8,128)(2,1)} %get-tuple-element.4) | data formatting | bytes 65536
  43.6 1.3 %copy.12 = f32[32,128]{1,0:T(8,128)} copy(f32[32,128]{1,0:T(8,128)} %get-tuple-element.5) | data formatting | bytes 32768

commit v4 on v3

--- a/solution.py
+++ b/solution.py
@@ -12,6 +12,7 @@
 STEPS = 4
 CHUNKS = 8
 AHEAD = 4
+FAR_FIRST = (2, 1, 3, 0)
 GREET = 1
 QROWS, QCOLS = 32, 512
 TOP = 32767.0
@@ -93,20 +94,23 @@
     q_y = (y % 2) * 2 + zh
     q_targets = [(z * 8 + q_y * 2 + 1 - core, zl * 2 + y // 2) for z in range(NZ)]
     q_sources = [(x * 8 + (zh * 2 + y // 2) * 2 + 1 - core, z * 2 + y % 2) for z in range(NX)]
-    row_sources = [(z * 8 + x * 2 + core, zl * 2 + (zh + crossed(z, zl)) % 2) for z in range(NZ)]
-    row_zh = (zh + crossed(zl, x)) % 2
-    self_row = x == zl
+    row_sources = [
+        (z * 8 + lax.rem(x - y - zl - z + 3 * NY, NY) * 2 + core, x * 2 + (zh + crossed(z, zl)) % 2) for z in range(NZ)
+    ]
+    row_peers = [
+        (zl * 8 + lax.rem(y + d, NY) * 2 + core, lax.rem(x + d, NX) * 2 + zh) for d in (1, 2, 3)
+    ]
+    self_row = x == 2 * ((zl + y) % 2)
     barrier = pltpu.get_barrier_semaphore()
 
     def signal(sem, devices):
         for device in devices:
             pl.semaphore_signal(sem, inc=1, device_id=device, device_id_type=MESH)
 
-    own_source = (x == zl) & (x == y)
-    signal(barrier, [*q_sources, z_peer, *x_peers, *y_peers, core_peer])
+    signal(barrier, [*q_sources, z_peer, *x_peers, *y_peers, core_peer, *row_peers])
     for z, device in enumerate(row_sources):
 
-        @pl.when(jnp.logical_not(own_source & (z == zl)))
+        @pl.when(jnp.logical_not(self_row & (z == zl)))
         def _(device=device):
             signal(barrier, [device])
 
@@ -138,8 +142,8 @@
             sigma_v[...] = jnp.broadcast_to(own_order(rows_v[...], dp), sigma_v.shape)
             sig_copy.start()
         if i == GREET:
-            pl.semaphore_wait(barrier, 16 - own_source.astype(jnp.int32))
-            signal(known_sem.at[0], y_peers)
+            pl.semaphore_wait(barrier, 19 - self_row.astype(jnp.int32))
+            signal(known_sem.at[0], row_peers)
             for z, device in enumerate(q_targets):
                 q_copies.append(
                     remote(queries, qall.at[1 - core, q_y, x], qs_sem.at[z], qr_sem.at[x], device)
@@ -148,8 +152,12 @@
 
     sig_copy.wait()
 
+    def store_z(k):
+        return lax.rem(zl + FAR_FIRST[k], NZ)
+
     def store_block(xx, k, h):
-        return xx * 8 + lax.rem(2 * k + h + dp, 8)
+        z = store_z(k)
+        return z * 8 + lax.rem(xx - y - zl - z + 3 * NY, NY) * 2 + (core + h) % 2
 
     def source(xx, k, h):
         return sigma_s[store_block(xx, k, h), 0]
@@ -204,12 +212,12 @@
             normed = kron * (1.0 / jnp.sqrt(mean + 1e-06))
             bsend[2 * k + h] = normed.reshape(R * R // 128, 128).astype(jnp.bfloat16)
         for h in range(2):
-            q = store_block(x, k, h)
+            q, near = store_block(x, k, h), (zh + crossed(zl, store_z(k))) % 2
             row = bsend.at[2 * k + h]
             for d in (2, 1, 3, 0):
                 n = (2 * k + h) * NX + d
-                copy = remote(row, brecv.at[dp], bs_sem.at[n], br_sem, (q, lax.rem(x + d, NX) * 2 + row_zh))
-                if k == 0 and h == 0 and d == 0:
+                copy = remote(row, brecv.at[dp], bs_sem.at[n], br_sem, (q, lax.rem(x + d, NX) * 2 + near))
+                if FAR_FIRST[k] == 0 and h == 0 and d == 0:
 
                     @pl.when(self_row)
                     def _(row=row):

time: 45.2 us -> 42.8 us (0.947)
  Pallas kernels: 41.6 us -> 39.3 us
    pallas_call x1, Pallas kernels: 41.6 us -> 39.3 us  [per_device(): pl.pallas_call(kernel, out_shape=(jax.ShapeDtypeStruct((SEQ, QCOLS), bf16...]
where the time goes in v4:
time: 42.8 us; the launch traced here: 42.6 us
  Pallas kernels  39.3 us (92%)
  local copies, waits for them, and re-layouts  2.7 us (6%)
  between operations  0.64 us (1%)
    pallas_call x1, Pallas kernels, per_device(): pl.pallas_call(kernel, out_shape=(jax.ShapeDtypeStruct((SEQ, QCOLS), bf16...  39.3 us
    unnamed x2, local copies, waits for them, and re-layouts  2.7 us

profile of v4, /device:TPU:1, one launch (start us, length us, event | category | flops | bytes accessed | tf_op | source)
XLA Modules:
  0.0 42.6 jit_solution(6407867410666421518)
XLA Ops:
  0.6 39.3 %shard_map.86 = (bf16[32,512]{1,0:T(8,128)(2,1)}, f32[32,128]{1,0:T(8,128)}) custom-call(bf16[2048,1792]{1,0:T(8,128)(2,1)} %hid.1, bf16[2048,512]{1,0:T(8,128)(2,1)} %grad.1, bf16[64,1792]{1,0:T(8,128)(2,1)} %bitcast.3, bf16[64,512]{1,0:T(8,128)(2,1)} %bitcast.4, s32[32]{0:T(128)} %lens_in.1, s32[8,128]{1,0:T(8,128)} %bitcast.5, bf16[32,512]{1,0:T(8,128)(2,1)} %queries.1), custom_call_target="tpu_custom_call" | custom-call | tf_op jit(solution)/shard_map/pallas_call | solution.py:299
  39.9 1.4 %copy.11 = bf16[32,512]{1,0:T(8,128)(2,1)} copy(bf16[32,512]{1,0:T(8,128)(2,1)} %get-tuple-element.4) | data formatting | bytes 65536
  41.3 1.3 %copy.12 = f32[32,128]{1,0:T(8,128)} copy(f32[32,128]{1,0:T(8,128)} %get-tuple-element.5) | data formatting | bytes 32768

commit v5 on v4

--- a/solution.py
+++ b/solution.py
@@ -11,9 +11,8 @@
 SEQ, LEN, R = 32, 64, 64
 STEPS = 4
 CHUNKS = 8
-AHEAD = 4
 FAR_FIRST = (2, 1, 3, 0)
-GREET = 1
+GREET, CUTS = (0, 3, 7), (6, 4)
 QROWS, QCOLS = 32, 512
 TOP = 32767.0
 
@@ -83,9 +82,13 @@
             pltpu.make_async_copy(hid.at[at], hid_v.at[at], hid_sem.at[i]),
             pltpu.make_async_copy(grad.at[at], grad_v.at[at], grad_sem.at[i]),
         ))
-    for i, pair in enumerate(chunk_loads[:AHEAD]):
-        for load in pair:
-            load.start(priority=int(i > 0))
+    def load_chunks(first, last):
+        for pair in chunk_loads[first:last]:
+            for load in pair:
+                load.start(priority=int(first > 0))
+
+    load_chunks(0, 1)
+    load_chunks(1, 4)
 
     x_peers = [(dp, lax.rem(x + d, NX) * 2 + zh) for d in (1, 2, 3)]
     z_peer = (dp, x * 2 + 1 - zh)
@@ -107,13 +110,16 @@
         for device in devices:
             pl.semaphore_signal(sem, inc=1, device_id=device, device_id_type=MESH)
 
-    signal(barrier, [*q_sources, z_peer, *x_peers, *y_peers, core_peer, *row_peers])
+    signal(barrier, [z_peer, *q_sources])
     for z, device in enumerate(row_sources):
 
         @pl.when(jnp.logical_not(self_row & (z == zl)))
         def _(device=device):
             signal(barrier, [device])
 
+    load_chunks(4, 6)
+    signal(barrier, [*x_peers, *y_peers, core_peer, *row_peers])
+    load_chunks(6, CHUNKS)
     sig_copy = pltpu.make_async_copy(sigma_v, sigma_s, sig_sem)
     loads[1].wait()
     for load in loads[2:]:
@@ -121,15 +127,20 @@
     wide_in[...] = jnp.concatenate([win_v[...], jnp.zeros_like(win_v)], axis=0).T
     wide_out[...] = jnp.concatenate([jnp.zeros_like(wout_v), wout_v[...]], axis=0).T
 
-    q_copies = []
+    q_copies = [
+        remote(queries, qall.at[1 - core, q_y, x], qs_sem.at[z], qr_sem.at[x], device)
+        for z, device in enumerate(q_targets)
+    ]
+    def ring(at, size):
+        return jnp.minimum(at, size - at)
+
+    hops = ring(x, NX) + ring(y, NY) + ring(zh * NZ + zl, 2 * NZ)
+    turns = [hops >= CUTS[0], (hops < CUTS[0]) & (hops >= CUTS[1]), hops < CUTS[1]]
     position = lax.broadcasted_iota(jnp.int32, (LEN, 2 * R), 0)
     for i in range(CHUNKS):
         at = pl.ds(i * tokens, tokens)
         for load in chunk_loads[i]:
             load.wait()
-        if i + AHEAD < CHUNKS:
-            for load in chunk_loads[i + AHEAD]:
-                load.start(priority=1)
         out = jnp.dot(hid_v[at, :], wide_in[...], preferred_element_type=jnp.float32)
         out += jnp.dot(grad_v[at, :], wide_out[...], preferred_element_type=jnp.float32)
         for j in range(tokens // LEN):
@@ -141,14 +152,15 @@
             loads[0].wait()
             sigma_v[...] = jnp.broadcast_to(own_order(rows_v[...], dp), sigma_v.shape)
             sig_copy.start()
-        if i == GREET:
-            pl.semaphore_wait(barrier, 19 - self_row.astype(jnp.int32))
-            signal(known_sem.at[0], row_peers)
-            for z, device in enumerate(q_targets):
-                q_copies.append(
-                    remote(queries, qall.at[1 - core, q_y, x], qs_sem.at[z], qr_sem.at[x], device)
-                )
-                q_copies[-1].start()
+        for turn, here in enumerate(turns):
+            if i == GREET[turn]:
+
+                @pl.when(here)
+                def _():
+                    pl.semaphore_wait(barrier, 19 - self_row.astype(jnp.int32))
+                    signal(known_sem.at[0], row_peers)
+                    for copy in q_copies:
+                        copy.start()
 
     sig_copy.wait()
 
@@ -163,14 +175,6 @@
         return sigma_s[store_block(xx, k, h), 0]
 
     x_copies, xc_copies = {}, []
-    for d in (2, 1, 3):
-        for k in range(STEPS):
-            for h in range(2):
-                s = source(lax.rem(x + d, NX), k, h)
-                xsscale[d - 1, 2 * k + h : 2 * k + h + 1, :] = scale[pl.ds(s, 1), :]
-        copy = remote(xsscale.at[d - 1], xrscale.at[d - 1], xcs_sem.at[d - 1], xcr_sem.at[d - 1], x_peers[d - 1])
-        copy.start()
-        xc_copies.append(copy)
     for k in range(STEPS):
         for d in (2, 1, 3):
             for h in range(2):
@@ -179,6 +183,16 @@
             copy = remote(xsend.at[d - 1, k], xrecv.at[d - 1, k], xs_sem.at[n], xr_sem.at[n], x_peers[d - 1])
             copy.start()
             x_copies[k, d] = copy
+        for d in (2, 1, 3) if k == 0 else ():
+            for kk in range(STEPS):
+                for h in range(2):
+                    s = source(lax.rem(x + d, NX), kk, h)
+                    xsscale[d - 1, 2 * kk + h : 2 * kk + h + 1, :] = scale[pl.ds(s, 1), :]
+            copy = remote(
+                xsscale.at[d - 1], xrscale.at[d - 1], xcs_sem.at[d - 1], xcr_sem.at[d - 1], x_peers[d - 1]
+            )
+            copy.start()
+            xc_copies.append(copy)
 
     for copy in xc_copies:
         copy.wait_recv()
@@ -234,13 +248,20 @@
 
     first_copy = []
     z_step(0)
+    z_step(1)
     mine = qall.at[core, y]
     for i in range(NX):
         pltpu.make_async_copy(queries, mine.at[i], qr_sem.at[i]).wait()
     for d, device in enumerate(y_peers):
         q_copies.append(remote(mine, mine, qs_sem.at[4 + d], qr_sem.at[4 + d], device))
         q_copies[-1].start()
-    z_step(1)
+
+    def to_core(d):
+        block = qall.at[core, lax.rem(y + d, NY)]
+        q_copies.append(remote(block, block, qs_sem.at[7 + d], qr_sem.at[7 + d], core_peer))
+        q_copies[-1].start()
+
+    to_core(0)
     pl.semaphore_wait(known_sem.at[0], 3)
     signal(known_sem.at[1], [core_peer])
     z_step(2)
@@ -248,16 +269,23 @@
     pl.semaphore_wait(known_sem.at[1], 1)
     for k in range(STEPS):
         b_step(k)
-    for copy in q_copies[4:]:
-        copy.wait_recv()
-    mine = qall.at[core]
-    q_copies.append(remote(mine, mine, qs_sem.at[7], qr_sem.at[7], core_peer))
-    q_copies[-1].start()
+    for d in (1, 3, 2):
+        block = qall.at[core, lax.rem(y + d, NY)]
+        remote(block, block, qs_sem.at[3 + d], qr_sem.at[7 - d], core_peer).wait_recv()
+        to_core(d)
 
     holder, _, block, row = tables(rows_v[...])
     slot = pick(holder, row, block == dp)
     place = lax.broadcasted_iota(jnp.int32, (DP, SEQ), 1) == slot
-    q_copies[-1].wait_recv()
+    for copy in q_copies[-4:]:
+        copy.wait_recv()
+
+    for copy in [*q_copies, *xc_copies, *x_copies.values(), *z_copies, *zc_copies, *b_copies]:
+        copy.wait_send()
+
+    @pl.when(jnp.logical_not(self_row))
+    def _():
+        first_copy[0].wait_send()
 
     pltpu.make_async_copy(brecv, brecv, br_sem).wait()
     flat[...] = brecv[...].reshape(flat.shape).astype(jnp.float32)
@@ -282,12 +310,10 @@
         precision=lax.Precision.HIGHEST, preferred_element_type=jnp.float32,
     ) * (1.0 / R)
 
-    for copy in [*q_copies, *xc_copies, *x_copies.values(), *z_copies, *zc_copies, *b_copies]:
-        copy.wait_send()
-
-    @pl.when(jnp.logical_not(self_row))
-    def _():
-        first_copy[0].wait_send()
+
+def hand_over(store_in, scores_in, store_ref, scores_ref):
+    store_ref[...] = store_in[...]
+    scores_ref[...] = scores_in[...]
 
 
 def per_device(hidden_in, grad_out, proj_in, proj_out, lengths, store_row, queries):
@@ -296,7 +322,7 @@
     bf16, f32, i16, i32 = jnp.bfloat16, jnp.float32, jnp.int16, jnp.int32
     tokens, wide_k = hidden_in.shape
     narrow_k = grad_out.shape[1]
-    return pl.pallas_call(
+    results = pl.pallas_call(
         kernel,
         out_shape=(
             jax.ShapeDtypeStruct((SEQ, QCOLS), bf16),
@@ -320,10 +346,17 @@
             dma((4,)), dma((CHUNKS,)), dma((CHUNKS,)), dma,
             dma((3 * STEPS,)), dma((3 * STEPS,)), dma((3,)), dma((3,)),
             dma((STEPS,)), dma((STEPS,)), dma((STEPS,)), dma((STEPS,)),
-            dma((2 * STEPS * NX,)), dma, dma((8,)), dma((8,)), pltpu.SemaphoreType.REGULAR((2,)),
+            dma((2 * STEPS * NX,)), dma, dma((11,)), dma((11,)), pltpu.SemaphoreType.REGULAR((2,)),
         ],
         compiler_params=pltpu.CompilerParams(collective_id=0, has_side_effects=True, vmem_limit_bytes=63 * 2**20),
     )(hidden_in, grad_out, proj_in.T, proj_out.T, lengths, rows, queries)
+    whole = pl.BlockSpec(memory_space=vmem)
+    return pl.pallas_call(
+        hand_over,
+        out_shape=tuple(jax.ShapeDtypeStruct(r.shape, r.dtype) for r in results),
+        in_specs=[whole] * 2,
+        out_specs=(whole,) * 2,
+    )(*results)
 
 
 def solution(mesh):

time: 42.8 us -> 41.3 us (0.965)
  local copies, waits for them, and re-layouts: 2.7 us -> 0 us
  Pallas kernels: 39.3 us -> 40.3 us
    unnamed x2 -> x0, local copies, waits for them, and re-layouts: 2.7 us -> none
    pallas_call x0 -> x1, Pallas kernels: none -> 1.38 us  [per_device(): pl.pallas_call(hand_over, out_shape=tuple((jax.ShapeDtypeStruct(r.shape,...]
where the time goes in v5:
time: 41.3 us; the launch traced here: 40.9 us
  Pallas kernels  40.3 us (98%)
  between operations  0.64 us (2%)
    pallas_call x1, Pallas kernels, per_device(): pl.pallas_call(kernel, out_shape=(jax.ShapeDtypeStruct((SEQ, QCOLS), bf16...  38.9 us
    pallas_call x1, Pallas kernels, per_device(): pl.pallas_call(hand_over, out_shape=tuple((jax.ShapeDtypeStruct(r.shape,...  1.38 us

profile of v5, /device:TPU:1, one launch (start us, length us, event | category | flops | bytes accessed | tf_op | source)
XLA Modules:
  0.0 40.9 jit_solution(17641921562439881580)
XLA Ops:
  0.6 38.9 %shard_map.86 = (bf16[32,512]{1,0:T(8,128)(2,1)}, f32[32,128]{1,0:T(8,128)}) custom-call(bf16[2048,1792]{1,0:T(8,128)(2,1)} %hid.1, bf16[2048,512]{1,0:T(8,128)(2,1)} %grad.1, bf16[64,1792]{1,0:T(8,128)(2,1)} %bitcast.3, bf16[64,512]{1,0:T(8,128)(2,1)} %bitcast.4, s32[32]{0:T(128)} %lens_in.1, s32[8,128]{1,0:T(8,128)} %bitcast.5, bf16[32,512]{1,0:T(8,128)(2,1)} %queries.1), custom_call_target="tpu_custom_call" | custom-call | tf_op jit(solution)/shard_map/pallas_call | solution.py:325
  39.5 1.4 %shard_map.87 = (bf16[32,512]{1,0:T(8,128)(2,1)}, f32[32,128]{1,0:T(8,128)}) custom-call(bf16[32,512]{1,0:T(8,128)(2,1)} %get-tuple-element.4.store_in, f32[32,128]{1,0:T(8,128)} %get-tuple-element.5.scores_in), custom_call_target="tpu_custom_call" | custom-call | tf_op jit(solution)/shard_map/pallas_call | solution.py:354

commit v6 on v5

--- a/solution.py
+++ b/solution.py
@@ -95,8 +95,9 @@
     y_peers = [(zl * 8 + lax.rem(y + d, NY) * 2 + core, tn) for d in (1, 2, 3)]
     core_peer = (zl * 8 + y * 2 + 1 - core, tn)
     q_y = (y % 2) * 2 + zh
-    q_targets = [(z * 8 + q_y * 2 + 1 - core, zl * 2 + y // 2) for z in range(NZ)]
-    q_sources = [(x * 8 + (zh * 2 + y // 2) * 2 + 1 - core, z * 2 + y % 2) for z in range(NX)]
+    q_targets = [((x % 2 + z) * 8 + q_y * 2 + 1 - core, zl * 2 + y // 2) for z in (0, 2)]
+    q_sources = [(x * 8 + (zh * 2 + y // 2) * 2 + 1 - core, (zl % 2 + z) * 2 + y % 2) for z in (0, 2)]
+    q_partner = ((zl + 1 - 2 * (zl % 2)) * 8 + y * 2 + core, tn)
     row_sources = [
         (z * 8 + lax.rem(x - y - zl - z + 3 * NY, NY) * 2 + core, x * 2 + (zh + crossed(z, zl)) % 2) for z in range(NZ)
     ]
@@ -110,7 +111,7 @@
         for device in devices:
             pl.semaphore_signal(sem, inc=1, device_id=device, device_id_type=MESH)
 
-    signal(barrier, [z_peer, *q_sources])
+    signal(barrier, [z_peer, *q_sources, q_partner])
     for z, device in enumerate(row_sources):
 
         @pl.when(jnp.logical_not(self_row & (z == zl)))
@@ -127,8 +128,9 @@
     wide_in[...] = jnp.concatenate([win_v[...], jnp.zeros_like(win_v)], axis=0).T
     wide_out[...] = jnp.concatenate([jnp.zeros_like(wout_v), wout_v[...]], axis=0).T
 
+    q_pos = (x % 2) * 2 + x // 2
     q_copies = [
-        remote(queries, qall.at[1 - core, q_y, x], qs_sem.at[z], qr_sem.at[x], device)
+        remote(queries, qall.at[1 - core, q_y, q_pos], qs_sem.at[z], qr_sem.at[x // 2], device)
         for z, device in enumerate(q_targets)
     ]
     def ring(at, size):
@@ -157,7 +159,7 @@
 
                 @pl.when(here)
                 def _():
-                    pl.semaphore_wait(barrier, 19 - self_row.astype(jnp.int32))
+                    pl.semaphore_wait(barrier, 18 - self_row.astype(jnp.int32))
                     signal(known_sem.at[0], row_peers)
                     for copy in q_copies:
                         copy.start()
@@ -248,10 +250,18 @@
 
     first_copy = []
     z_step(0)
+    half = qall.at[core, y, pl.ds((zl % 2) * 2, 2)]
+    for i in range(2):
+        pltpu.make_async_copy(queries, half.at[i], qr_sem.at[i]).wait()
+    q_copies.append(remote(half, half, qs_sem.at[11], qr_sem.at[11], q_partner))
+    q_copies[-1].start()
     z_step(1)
+    pl.semaphore_wait(known_sem.at[0], 3)
+    signal(known_sem.at[1], [core_peer])
+    z_step(2)
+    z_step(3)
+    q_copies[2].wait_recv()
     mine = qall.at[core, y]
-    for i in range(NX):
-        pltpu.make_async_copy(queries, mine.at[i], qr_sem.at[i]).wait()
     for d, device in enumerate(y_peers):
         q_copies.append(remote(mine, mine, qs_sem.at[4 + d], qr_sem.at[4 + d], device))
         q_copies[-1].start()
@@ -262,10 +272,6 @@
         q_copies[-1].start()
 
     to_core(0)
-    pl.semaphore_wait(known_sem.at[0], 3)
-    signal(known_sem.at[1], [core_peer])
-    z_step(2)
-    z_step(3)
     pl.semaphore_wait(known_sem.at[1], 1)
     for k in range(STEPS):
         b_step(k)
@@ -300,7 +306,7 @@
     total = jnp.zeros((DP, 4 * QROWS), jnp.float32)
     for c in range(TP):
         block = jnp.concatenate(
-            [qall[1 - m % 2, (m // 2) * 2 + c % 2, c // 2] for m in range(4)], axis=0
+            [qall[1 - m % 2, (m // 2) * 2 + c % 2, (c // 2 % 2) * 2 + c // 4] for m in range(4)], axis=0
         )
         total += lax.dot_general(
             wide[:, c * QCOLS : (c + 1) * QCOLS], block, (((1,), (1,)), ((), ())), preferred_element_type=jnp.float32
@@ -346,7 +352,7 @@
             dma((4,)), dma((CHUNKS,)), dma((CHUNKS,)), dma,
             dma((3 * STEPS,)), dma((3 * STEPS,)), dma((3,)), dma((3,)),
             dma((STEPS,)), dma((STEPS,)), dma((STEPS,)), dma((STEPS,)),
-            dma((2 * STEPS * NX,)), dma, dma((11,)), dma((11,)), pltpu.SemaphoreType.REGULAR((2,)),
+            dma((2 * STEPS * NX,)), dma, dma((12,)), dma((12,)), pltpu.SemaphoreType.REGULAR((2,)),
         ],
         compiler_params=pltpu.CompilerParams(collective_id=0, has_side_effects=True, vmem_limit_bytes=63 * 2**20),
     )(hidden_in, grad_out, proj_in.T, proj_out.T, lengths, rows, queries)

time: 41.3 us -> 39.9 us (0.966)
  the two profiles are of different devices: /device:TPU:1 before, /device:TPU:9 now
where the time goes in v6:
time: 39.9 us; the launch traced here: 39.8 us
  Pallas kernels  39.2 us (98%)
  between operations  0.64 us (2%)
    pallas_call x1, Pallas kernels, per_device(): pl.pallas_call(kernel, out_shape=(jax.ShapeDtypeStruct((SEQ, QCOLS), bf16...  37.8 us
    pallas_call x1, Pallas kernels, per_device(): pl.pallas_call(hand_over, out_shape=tuple((jax.ShapeDtypeStruct(r.shape,...  1.38 us

profile of v6, /device:TPU:9, one launch (start us, length us, event | category | flops | bytes accessed | tf_op | source)
XLA Modules:
  0.0 39.8 jit_solution(4012152834150807132)
XLA Ops:
  0.6 37.8 %shard_map.86 = (bf16[32,512]{1,0:T(8,128)(2,1)}, f32[32,128]{1,0:T(8,128)}) custom-call(bf16[2048,1792]{1,0:T(8,128)(2,1)} %hid.1, bf16[2048,512]{1,0:T(8,128)(2,1)} %grad.1, bf16[64,1792]{1,0:T(8,128)(2,1)} %bitcast.3, bf16[64,512]{1,0:T(8,128)(2,1)} %bitcast.4, s32[32]{0:T(128)} %lens_in.1, s32[8,128]{1,0:T(8,128)} %bitcast.5, bf16[32,512]{1,0:T(8,128)(2,1)} %queries.1), custom_call_target="tpu_custom_call" | custom-call | tf_op jit(solution)/shard_map/pallas_call | solution.py:331
  38.4 1.4 %shard_map.87 = (bf16[32,512]{1,0:T(8,128)(2,1)}, f32[32,128]{1,0:T(8,128)}) custom-call(bf16[32,512]{1,0:T(8,128)(2,1)} %get-tuple-element.4.store_in, f32[32,128]{1,0:T(8,128)} %get-tuple-element.5.scores_in), custom_call_target="tpu_custom_call" | custom-call | tf_op jit(solution)/shard_map/pallas_call | solution.py:360
